TPU v7x, 32 devices: a whole 2x2x4 slice. The times are simulated.
32 devices in a mesh: tm: 8 (over z, x), sta: 4 (over y, core).
Axes of the slice: x: 2, y: 2, z: 4, core: 2. Of those that a mesh axis runs over, the one named last changes fastest.
Arguments:
- voltages: bfloat16 [2, 4, 64, 262144], P(None, None, 'sta', 'tm'), may hold values from -6 to 6
- sample_delay: int32 [64, 8], P('sta', 'tm'), may hold values from 0 to 8192, as said below
- frac_index: int32 [64, 8], P('sta', 'tm'), may hold values from 0 to 63
- phase_index: int32 [4, 64, 8], P(None, 'sta', 'tm'), may hold values from 0 to 1023
- fringe_rate: float32 [4, 64], P(None, 'sta'), may hold values from -3 to 3
Outputs:
- visibilities: float32 [4, 16384, 64, 128], P(None, ('tm', 'sta'))
Inputs may be any that keep to these rules, and one draw needn't show every extreme that they name: `sample_delay`: the largest delay, 8192, occurs in every draw.
All inputs are finite; a program needn't handle non-finite values.
Results may differ from a plain program's by a relative error of at most 0.0089.
Values may be sent and summed in bfloat16 or wider, within the bound.
A program may use at most 256 MiB of HBM per device.

v0:
```python
import math

import jax
import jax.numpy as jnp
from jax import lax
from jax.sharding import PartitionSpec as P

CHANNELS = 16384
RADIX_A = 128
RADIX_B = 128
TAPS = 32
NFRAC = 64
NPHASE = 1024
MAXD = 8192


def shifted(value, axis, steps):
    count = lax.axis_size(axis)
    first, last = (max(0, -steps), min(count, count - steps))
    return lax.ppermute(value, axis, [(source, source + steps) for source in range(first, last)])


def toeplitz_of(fraction_index):
    inputs_at = jnp.arange(256, dtype=jnp.int32)
    outputs_at = jnp.arange(128, dtype=jnp.int32)
    distance = inputs_at[:, None] - outputs_at[None, :]
    inside = (distance >= 0) & (distance < TAPS)
    fraction = fraction_index.astype(jnp.float32) / NFRAC
    offset = distance.astype(jnp.float32)
    centre = offset[None, :, :] - (TAPS // 2 - 1) - fraction[:, None, None]
    window_taper = 0.5 - 0.5 * jnp.cos(2.0 * jnp.pi * (offset + 0.5) / TAPS)
    values = jnp.sinc(centre) * window_taper[None, :, :]
    return jnp.where(inside[None, :, :], values, 0.0).astype(jnp.bfloat16)


def filter_rows(source, starts, kernel, sample_count):
    slicer = jax.vmap(
        lambda series, start_at: lax.dynamic_slice_in_dim(
            series, start_at, sample_count + 128, axis=1
        ),
        in_axes=(1, 0),
        out_axes=1,
    )
    pieces = slicer(source, starts)
    row_count = pieces.shape[1]
    blocks = sample_count // 128
    tiles = pieces.reshape(2, row_count, blocks + 1, 128)
    upper = jnp.einsum(
        "crnp,rpv->crnv", tiles[:, :, :blocks], kernel[:, :128], preferred_element_type=jnp.float32
    )
    lower = jnp.einsum(
        "crnp,rpv->crnv", tiles[:, :, 1:], kernel[:, 128:], preferred_element_type=jnp.float32
    )
    return (upper + lower).reshape(2, row_count, sample_count)


def rotate_rows(filtered, phase_rows, rate_rows, slice_length):
    sample_count = filtered.shape[-1]
    position = jnp.arange(sample_count, dtype=jnp.int32).astype(jnp.float32) / slice_length
    cycles = (
        phase_rows.astype(jnp.float32)[:, None] / NPHASE + rate_rows[:, None] * position[None, :]
    )
    phase_angle = 2.0 * jnp.pi * cycles
    cosine = jnp.cos(phase_angle)
    sine_value = jnp.sin(phase_angle)
    real_part = filtered[0] * cosine + filtered[1] * sine_value
    imag_part = filtered[1] * cosine - filtered[0] * sine_value
    return jnp.stack([real_part, imag_part]).astype(jnp.bfloat16)


def rotation_table(indices, radix_size):
    product = indices[:, None] * indices[None, :] % radix_size
    table_angle = product.astype(jnp.float32) * (2.0 * math.pi / radix_size)
    scaling = 1.0 / math.sqrt(radix_size)
    cosine = jnp.cos(table_angle) * scaling
    sine_value = jnp.sin(table_angle) * scaling
    stacked = jnp.stack(
        [jnp.stack([cosine, sine_value], axis=1), jnp.stack([-sine_value, cosine], axis=1)], axis=0
    )
    return stacked.astype(jnp.bfloat16)


def dft_tables():
    along_a = jnp.arange(RADIX_A, dtype=jnp.int32)
    along_b = jnp.arange(RADIX_B, dtype=jnp.int32)
    first_table = rotation_table(along_a, RADIX_A)
    second_table = rotation_table(along_b, RADIX_B)
    product = along_a[:, None] * along_b[None, :] % CHANNELS
    twist_angle = product.astype(jnp.float32) * (2.0 * math.pi / CHANNELS)
    twiddle = jnp.stack([jnp.cos(twist_angle), jnp.sin(twist_angle)])
    return (first_table, twiddle, second_table)


def transform(rotated, tables, block_width):
    first_table, twiddle, second_table = tables
    row_count = rotated.shape[1]
    frames = rotated.shape[2] // CHANNELS
    arranged = rotated.reshape(2, row_count, frames, RADIX_A, RADIX_B)
    section_half = jnp.einsum(
        "pkcn,crfnm->prfkm", first_table, arranged, preferred_element_type=jnp.float32
    )
    real_part = section_half[0] * twiddle[0] + section_half[1] * twiddle[1]
    imag_part = section_half[1] * twiddle[0] - section_half[0] * twiddle[1]
    partial_value = jnp.stack([real_part, imag_part]).astype(jnp.bfloat16)
    block_count = CHANNELS // block_width
    if block_width <= RADIX_A:
        split_rows = partial_value.reshape(
            2, row_count, frames, RADIX_A // block_width, block_width, RADIX_B
        )
        spectrum = jnp.einsum(
            "qjpm,prfakm->rfjaqk", second_table, split_rows, preferred_element_type=jnp.float32
        )
    else:
        split_table = second_table.reshape(2, block_count, block_width // RADIX_A, 2, RADIX_B)
        spectrum = jnp.einsum(
            "qJjpm,prfkm->rfJqjk", split_table, partial_value, preferred_element_type=jnp.float32
        )
    return spectrum.astype(jnp.bfloat16).reshape(row_count, frames, block_count, 2 * block_width)


def correlate(spectra):
    frame_total = spectra.shape[2]
    turned = jnp.stack([-spectra[:, :, :, 1], spectra[:, :, :, 0]], axis=3)
    partner = jnp.concatenate([spectra, turned], axis=1)
    summed = jnp.einsum("bifck,bjfck->bkij", spectra, partner, preferred_element_type=jnp.float32)
    return summed / frame_total


def local(voltages, sample_delay, frac_index, phase_index, fringe_rate):
    band_count = voltages.shape[1]
    station_count = voltages.shape[2]
    length = voltages.shape[3]
    frames = length // CHANNELS
    row_count = band_count * station_count
    flattened = voltages.reshape(2, row_count, length)
    delays = jnp.broadcast_to(sample_delay[:, 0][None, :], (band_count, station_count)).reshape(
        row_count
    )
    kernel = toeplitz_of(frac_index[:, 0])
    kernel_rows = jnp.broadcast_to(kernel[None], (band_count,) + kernel.shape).reshape(
        (row_count,) + kernel.shape[1:]
    )
    phase_rows = phase_index[:, :, 0].reshape(row_count)
    rate_rows = fringe_rate.reshape(row_count)
    rim_width = MAXD + TAPS - 1
    following = shifted(flattened[:, :, :rim_width], "tm", -1)
    padding = jnp.zeros((2, row_count, 129 - TAPS), flattened.dtype)
    source = jnp.concatenate([flattened, following, padding], axis=2)
    rotated = rotate_rows(
        filter_rows(source, delays, kernel_rows, length), phase_rows, rate_rows, length
    )
    slices = lax.axis_size("tm")
    groups = lax.axis_size("sta")
    block_width = CHANNELS // (slices * groups)
    spectra = transform(rotated, dft_tables(), block_width)
    packed = spectra.reshape(band_count, station_count, frames, slices, groups, 2 * block_width)
    received = lax.all_to_all(
        lax.all_to_all(packed, "tm", split_axis=3, concat_axis=2, tiled=True),
        "sta",
        split_axis=4,
        concat_axis=1,
        tiled=True,
    )
    gathered = received.reshape(band_count, station_count * groups, slices * frames, 2, block_width)
    return correlate(gathered)


def solution(mesh):
    return jax.shard_map(
        local,
        mesh=mesh,
        in_specs=(
            P(None, None, "sta", "tm"),
            P("sta", "tm"),
            P("sta", "tm"),
            P(None, "sta", "tm"),
            P(None, "sta"),
        ),
        out_specs=P(None, ("tm", "sta"), None, None),
        check_vma=False,
    )
```

profile of v0, /device:TPU:11, one launch (start us, length us, event | category | flops | bytes accessed | tf_op | source)
XLA Modules:
  0.0 949.3 jit_solution(5046426309771215276)
XLA Ops:
  0.0 14.6 %copy.28 = bf16[2,4,16,32768]{3,0,2,1:T(2,128)(2,1)S(1)} copy(bf16[2,4,16,32768]{3,2,1,0:T(8,128)(2,1)} %param.5) | data formatting | bytes 16777216 | tf_op args[0]
  33.0 34.7 %collective-permute-done = bf16[2,64,8223]{2,0,1:T(2,128)(2,1)S(1)} collective-permute-done((bf16[2,64,8223]{2,0,1:T(2,128)(2,1)}, bf16[2,64,8223]{2,0,1:T(2,128)(2,1)S(1)}, u32[]{:S(2)}, u32[]{:S(2)}) %collective-permute-start) | collective-permute-done | bytes 2105120 | tf_op jit(solution)/shard_map/ppermute | solution.py:20
  67.8 60.9 %dynamic-update-slice.3 = bf16[2,64,41088]{2,0,1:T(2,128)(2,1)} dynamic-update-slice(bf16[2,64,41088]{2,0,1:T(2,128)(2,1)} %constant_dynamic-update-slice_fusion, bf16[2,64,8223]{2,0,1:T(2,128)(2,1)S(1)} %collective-permute-done, s32[]{} %constant.144, s32[]{} %constant.144, s32[]{} %constant.145) | dynamic-update-slice | bytes 4210180
  128.7 10.2 %dynamic-update-slice.4 = bf16[2,64,41088]{2,0,1:T(2,128)(2,1)} dynamic-update-slice(bf16[2,64,41088]{2,0,1:T(2,128)(2,1)} %dynamic-update-slice.3, bf16[2,64,97]{2,0,1:T(2,128)(2,1)S(1)} %broadcast_in_dim.25, s32[]{} %constant.144, s32[]{} %constant.144, s32[]{} %constant.146) | dynamic-update-slice | bytes 49668 | tf_op jit(solution)/shard_map/concatenate | solution.py:148
  138.9 234.9 %while.1 = (s32[]{:T(128)}, bf16[64,2,41088]{2,1,0:T(2,128)(2,1)}, s32[64,3]{0,1:T(4,128)S(1)}, bf16[64,2,32896]{2,1,0:T(2,128)(2,1)}, s32[]{:T(128)}) while((s32[]{:T(128)}, bf16[64,2,41088]{2,1,0:T(2,128)(2,1)}, s32[64,3]{0,1:T(4,128)S(1)}, bf16[64,2,32896]{2,1,0:T(2,128)(2,1)}, s32[]{:T(128)}) %tuple.32), condition=%wide.while_cond, body=%wide.while_body.sunk | while | flops 2 | bytes 264309 | solution.py:38
  373.7 14.2 %reshape.521 = bf16[2,64,257,128]{3,2,0,1:T(8,128)(2,1)} reshape(bf16[2,64,32896]{2,0,1:T(2,128)(2,1)} %bitcast.99) | data formatting | bytes 16842752 | tf_op jit(solution)/shard_map/reshape | solution.py:47
  390.4 11.9 %fusion.6 = f32[64,128,2,256]{3,1,2,0:T(8,128)} fusion(bf16[2,64,257,128]{3,2,0,1:T(8,128)(2,1)} %reshape.521, bf16[64,256,128]{1,2,0:T(8,128)(2,1)S(1)} %bitcast.97), kind=kOutput, calls=%fused_computation.13 | convolution fusion | flops 1073741824 | bytes 27262976 | tf_op jit(solution)/shard_map/crnp,rpv->crnv/dot_general | solution.py:48
  402.3 16.7 %add_bitcast_fusion = f32[2,64,256,128]{2,3,0,1:T(8,128)} fusion(f32[64,128,2,256]{3,1,2,0:T(8,128)} %fusion.6, bf16[2,64,257,128]{3,2,0,1:T(8,128)(2,1)} %reshape.521, bf16[64,256,128]{1,2,0:T(8,128)(2,1)} %bitcast.98), kind=kOutput, calls=%fused_computation.9 | convolution fusion | flops 1077936128 | bytes 44040192 | tf_op jit(solution)/shard_map/crnp,rpv->crnv/dot_general | solution.py:51
  419.0 11.1 %fusion.78 = (f32[1,64,256,128]{2,3,0,1:T(8,128)}, f32[1,64,256,128]{2,3,0,1:T(8,128)}) fusion(f32[2,64,256,128]{2,3,0,1:T(8,128)} %add_bitcast_fusion), kind=kLoop, calls=%fused_computation.130 | loop fusion | bytes 33554432 | tf_op jit(solution)/shard_map/slice | solution.py:66
  430.1 10.8 %squeeze.4 = f32[1,64,2,128,128]{3,2,4,1,0:T(2,128)} reshape(f32[1,64,256,128]{2,3,0,1:T(8,128)} %get-tuple-element.29) | data formatting | bytes 16777216 | tf_op jit(solution)/shard_map/squeeze | solution.py:66
  440.9 10.8 %squeeze.5 = f32[1,64,2,128,128]{3,2,4,1,0:T(2,128)} reshape(f32[1,64,256,128]{2,3,0,1:T(8,128)} %get-tuple-element.30) | data formatting | bytes 16777216 | tf_op jit(solution)/shard_map/squeeze | solution.py:66
  451.6 35.4 %add_convert_fusion.1 = (bf16[1,64,2,128,128]{3,4,0,2,1:T(8,128)(2,1)S(1)}, bf16[1,64,2,128,128]{3,4,0,2,1:T(8,128)(2,1)}) fusion(f32[1,64,2,128,128]{3,2,4,1,0:T(2,128)} %squeeze.5, f32[1,64,2,128,128]{3,2,4,1,0:T(2,128)} %squeeze.4, f32[2,128,128]{1,2,0:T(8,128)S(1)} %convert_multiply_fusion, f32[64]{0:T(128)S(1)} %mul.534, f32[64]{0:T(128)S(1)} %div.46), kind=kLoop, calls=%fused_computation.24 | loop fusion | flops 23068672 | bytes 25297408 | tf_op jit(solution)/shard_map/convert.16
  500.1 9.8 %copy.37 = bf16[64,2,32,2,4,128]{5,4,3,0,2,1:T(4,128)(2,1)} copy(bf16[64,2,32,2,4,128]{5,2,4,3,1,0:T(8,128)(2,1)S(1)} %fusion.14) | data formatting | bytes 16777216 | tf_op jit(solution)/shard_map/convert_element_type | solution.py:118
  509.9 14.3 %reshape_reshape.3 = bf16[4,16,2,8,4,1024]{5,1,0,4,3,2:T(8,128)(2,1)} reshape(bf16[64,2,32,2,4,128]{5,4,3,0,2,1:T(4,128)(2,1)} %copy.37) | data formatting | bytes 16777216 | tf_op jit(solution)/shard_map/reshape;reshape | solution.py:156
  524.2 8.7 copy.38
  532.9 185.7 %all_to_all.33 = bf16[4,16,2,8,4,1024]{5,1,0,4,2,3:T(8,128)(2,1)} all-to-all(bf16[4,16,2,8,4,1024]{5,1,0,4,2,3:T(8,128)(2,1)} %copy.38), channel_id=1, replica_groups=mesh['tm'=8,'sta'=4] {'tm'}, dimensions={3} | all-to-all | bytes 16777216 | tf_op jit(solution)/shard_map/all_to_all | solution.py:158
  718.6 8.7 copy.39
  727.3 8.5 copy.40
  735.8 102.1 %all_to_all.34 = bf16[4,16,16,1,4,1024]{5,1,2,0,3,4:T(8,128)(2,1)} all-to-all(bf16[4,16,16,1,4,1024]{5,1,2,0,3,4:T(8,128)(2,1)} %copy.40), channel_id=1, replica_groups=mesh['tm'=8,'sta'=4] {'sta'}, dimensions={4} | all-to-all | bytes 16777216 | tf_op jit(solution)/shard_map/all_to_all | solution.py:157
  837.9 12.8 %copy.41 = bf16[4,4,16,16,1,1,1024]{6,3,2,1,0,5,4:T(8,128)(2,1)} copy(bf16[4,4,16,16,1,1,1024]{6,2,3,0,1,5,4:T(8,128)(2,1)} %bitcast.96) | data formatting | bytes 16777216 | tf_op jit(solution)/shard_map/all_to_all | solution.py:157
  850.7 14.5 %reshape.488 = bf16[4,64,16,2,512]{4,3,2,1,0:T(2,128)(2,1)} reshape(bf16[4,4,16,16,1,1,1024]{6,3,2,1,0,5,4:T(8,128)(2,1)} %copy.41) | data formatting | bytes 16777216 | tf_op jit(solution)/shard_map/reshape | solution.py:164
  865.2 28.7 %copy.45 = bf16[4,64,16,2,512]{1,2,3,4,0:T(8,128)(2,1)} copy(bf16[4,64,16,2,512]{4,3,2,1,0:T(2,128)(2,1)} %reshape.488) | data formatting | bytes 16777216 | tf_op jit(solution)/shard_map/reshape | solution.py:164
  894.0 11.6 %slice_negate_fusion = (bf16[4,64,16,1,512]{1,2,3,4,0:T(8,128)(2,1)}, bf16[4,64,16,1,512]{1,2,3,4,0:T(8,128)(2,1)}) fusion(bf16[4,64,16,2,512]{1,2,3,4,0:T(8,128)(2,1)} %copy.45), kind=kLoop, calls=%fused_computation.11 | loop fusion | flops 2097152 | bytes 16777216 | tf_op jit(solution)/shard_map/neg | solution.py:123
  905.5 43.3 %bitcast_multiply_fusion = f32[4,512,64,128]{3,2,1,0:T(8,128)} fusion(bf16[4,64,16,2,512]{1,2,3,4,0:T(8,128)(2,1)} %copy.45, bf16[4,64,16,1,512]{1,2,3,4,0:T(8,128)(2,1)} %get-tuple-element.28, bf16[4,64,16,1,512]{1,2,3,4,0:T(8,128)(2,1)} %get-tuple-element.27), kind=kOutput, calls=%fused_computation.2 | convolution fusion | flops 1140850688 | bytes 83886080 | tf_op jit(solution)/shard_map/bifck,bjfck->bkij/dot_general | solution.py:125
  (236 shorter events, 268.5 us)
Async XLA Ops:
  17.6 50.2 %collective-permute-start = (bf16[2,64,8223]{2,0,1:T(2,128)(2,1)}, bf16[2,64,8223]{2,0,1:T(2,128)(2,1)S(1)}, u32[]{:S(2)}, u32[]{:S(2)}) collective-permute-start(bf16[2,64,8223]{2,0,1:T(2,128)(2,1)} %slice.65), channel_id=1, source_target_pairs={{4,0},{8,4},{12,8},{16,12},{20,16},{24,20},{28,24},{5,1},{9,5},{13... | collective-permute-start | bytes 6315272 | tf_op jit(solution)/shard_map/ppermute | solution.py:20
  19.9 7.0 copy-start.6
  19.9 7.1 copy-start.5
  19.9 7.2 copy-start.4
  20.0 9.3 copy-start.7
  388.4 2.0 copy-start
  451.6 35.5 %copy-start.1 = (bf16[1,128,2,128]{3,1,2,0:T(8,128)(2,1)S(1)}, bf16[1,128,2,128]{3,1,2,0:T(8,128)(2,1)}, u32[]{:S(2)}) copy-start(bf16[1,128,2,128]{3,1,2,0:T(8,128)(2,1)} %get-tuple-element.32) | copy-start | bytes 196612
  491.7 3.8 copy-start.2
  491.7 3.8 copy-start.3
where the time goes:
time: 966 us; the launch traced here: 949 us
  local copies, waits for them, and re-layouts  486 us (50%)
  blocking collectives  288 us (30%)
  matrix products  81 us (8%)
  other arithmetic  56.6 us (6%)
  waiting for transfers between devices  34.7 us (4%)
    gather x192, local copies, waits for them, and re-layouts  235 us
    all_to_all x1, blocking collectives, local(): lax.all_to_all(packed, 'tm', split_axis=3, concat_axis=2, tiled=True)  186 us
    all_to_all x1, blocking collectives, local(): lax.all_to_all(lax.all_to_all(packed, 'tm', split_axis=3, concat_axis=2,...  102 us
    unnamed x20, local copies, waits for them, and re-layouts  84.5 us
    dot_general x1, matrix products, correlate(): jnp.einsum('bifck,bjfck->bkij', spectra, partner, preferred_element_type=...  43.3 us
    reshape x2, local copies, waits for them, and re-layouts, local(): received.reshape(band_count, station_count * groups, slices * frames, 2,...  43.2 us
    another operation x5, other arithmetic  40.8 us
    ppermute x1, waiting for transfers between devices, shifted(): lax.ppermute(value, axis, [(source, source + steps) for source in range(f...  34.7 us
  transfers between devices with their start and end apart: 1, of which 1 were waited for; matrix products, arithmetic and copies ran while one was open for 1% of the time, Pallas kernels for 0%

commit v1 on v0

--- a/solution.py
+++ b/solution.py
@@ -1,8 +1,12 @@
+import functools
 import math
 
 import jax
 import jax.numpy as jnp
+import numpy as np
 from jax import lax
+from jax.experimental import pallas as pl
+from jax.experimental.pallas import tpu as pltpu
 from jax.sharding import PartitionSpec as P
 
 CHANNELS = 16384
@@ -126,7 +130,7 @@
     return summed / frame_total
 
 
-def local(voltages, sample_delay, frac_index, phase_index, fringe_rate):
+def local_wide(voltages, sample_delay, frac_index, phase_index, fringe_rate):
     band_count = voltages.shape[1]
     station_count = voltages.shape[2]
     length = voltages.shape[3]
@@ -165,6 +169,320 @@
     return correlate(gathered)
 
 
+ROWS = CHANNELS // 128
+REACH = MAXD // 128 + 1
+STRIDE = ROWS + REACH + 7
+WINDOW = 384
+MESH = pl.DeviceIdType.MESH
+
+
+def delay_filters(frac_index, remainder):
+    inputs_at = jnp.arange(WINDOW, dtype=jnp.int32)
+    outputs_at = jnp.arange(128, dtype=jnp.int32)
+    distance = inputs_at[None, :, None] - outputs_at[None, None, :] - remainder[:, None, None]
+    inside = (distance >= 0) & (distance < TAPS)
+    fraction = frac_index.astype(jnp.float32) / NFRAC
+    offset = distance.astype(jnp.float32)
+    centre = offset - (TAPS // 2 - 1) - fraction[:, None, None]
+    window_taper = 0.5 - 0.5 * jnp.cos(2.0 * jnp.pi * (offset + 0.5) / TAPS)
+    return jnp.where(inside, jnp.sinc(centre) * window_taper, 0.0).astype(jnp.bfloat16)
+
+
+def phasors(phase_index, fringe_rate, length):
+    starts = jnp.arange(length // 128, dtype=jnp.int32).astype(jnp.float32) * 128 / length
+    within = jnp.arange(128, dtype=jnp.int32).astype(jnp.float32) / length
+    start_angle = 2.0 * jnp.pi * (
+        phase_index.astype(jnp.float32)[..., None] / NPHASE + fringe_rate[..., None] * starts
+    )
+    within_angle = 2.0 * jnp.pi * (fringe_rate[..., None] * within)
+    coarse = jnp.stack([jnp.cos(start_angle), jnp.sin(start_angle)], axis=2)
+    fine = jnp.stack([jnp.cos(within_angle), jnp.sin(within_angle)], axis=2)
+    return coarse, fine
+
+
+def station_kernel(
+    whole_rows, head_ref, tail_ref, filter_ref, coarse_ref, fine_ref, first_ref, twiddle_ref,
+    second_ref, out_ref, series, gathered
+):
+    stations = head_ref.shape[2]
+
+    for part in range(2):
+        for row in range(ROWS + REACH):
+            if row < ROWS:
+                tile = head_ref[part, 0, :, row * 128 : (row + 1) * 128]
+            else:
+                tile = tail_ref[part, 0, :, (row - ROWS) * 128 : (row - ROWS + 1) * 128]
+            series[part, pl.ds(row, stations, stride=STRIDE), :] = tile.astype(jnp.float32)
+        series[part, pl.ds(ROWS + REACH, stations, stride=STRIDE), :] = jnp.zeros(
+            (stations, 128), jnp.float32
+        )
+
+    def across(row):
+        return jnp.transpose(jnp.broadcast_to(row, (128, 128)))
+
+    def one(station):
+        base = station * STRIDE + whole_rows[station]
+        parts = []
+        for part in range(2):
+            pieces = [
+                series[part, pl.ds(base + step, ROWS), :].astype(jnp.bfloat16) for step in range(3)
+            ]
+            parts.append(jnp.concatenate(pieces, axis=1))
+        filtered = jnp.dot(
+            jnp.concatenate(parts, axis=0), filter_ref[station], preferred_element_type=jnp.float32
+        )
+        coarse = coarse_ref[0, station]
+        fine = fine_ref[0, station]
+        cos_a, sin_a = across(coarse[0:1]), across(coarse[1:2])
+        cos_b, sin_b = fine[0:1], fine[1:2]
+        cosine = cos_a * cos_b - sin_a * sin_b
+        sine = sin_a * cos_b + cos_a * sin_b
+        re, im = filtered[:ROWS], filtered[ROWS:]
+        return jnp.concatenate(
+            [re * cosine + im * sine, im * cosine - re * sine], axis=0
+        ).astype(jnp.bfloat16)
+
+    def pair(at, carry):
+        rotated = jnp.concatenate([one(2 * at), one(2 * at + 1)], axis=1)
+        half = jnp.dot(first_ref[...], rotated, preferred_element_type=jnp.float32)
+        cosine, sine = twiddle_ref[0], twiddle_ref[1]
+        turned = []
+        for which in range(2):
+            re = half[:RADIX_A, which * 128 : (which + 1) * 128]
+            im = half[RADIX_A:, which * 128 : (which + 1) * 128]
+            turned.append(
+                jnp.concatenate([re * cosine + im * sine, im * cosine - re * sine], axis=1)
+            )
+        partial_value = jnp.concatenate(turned, axis=0).astype(jnp.bfloat16)
+        spectrum = lax.dot_general(
+            second_ref[...], partial_value, (((1,), (1,)), ((), ())),
+            preferred_element_type=jnp.float32,
+        )
+        for which in range(2):
+            gathered[pl.ds(2 * at + which, 2 * RADIX_B, stride=stations), :] = spectrum[
+                :, which * 128 : (which + 1) * 128
+            ]
+        return carry
+
+    lax.fori_loop(0, stations // 2, pair, 0)
+    blocks, inner = out_ref.shape[1], out_ref.shape[2]
+
+    def pack(block, carry):
+        rows = pl.ds(pl.multiple_of(block * inner, inner), inner)
+        out_ref[0, block] = gathered[rows, :].astype(jnp.bfloat16)
+        return carry
+
+    lax.fori_loop(0, blocks, pack, 0)
+
+
+def station_spectra(frame, voltages, tail, filters, coarse, fine, tables, whole_rows, blocks):
+    _, bands, stations, _ = voltages.shape
+    first, twiddle, second = tables
+    inner = 2 * RADIX_B // blocks * stations
+    whole = lambda shape: pl.BlockSpec(shape, lambda band, rows: (0,) * len(shape))
+    return pl.pallas_call(
+        station_kernel,
+        out_shape=jax.ShapeDtypeStruct((bands, blocks, inner, 128), jnp.bfloat16),
+        grid_spec=pltpu.PrefetchScalarGridSpec(
+            num_scalar_prefetch=1,
+            grid=(bands,),
+            in_specs=[
+                pl.BlockSpec((2, 1, stations, CHANNELS), lambda band, rows: (0, band, 0, frame)),
+                pl.BlockSpec((2, 1, stations, REACH * 128), lambda band, rows: (0, band, 0, 0)),
+                whole(filters.shape),
+                pl.BlockSpec((1, stations, 2, 128), lambda band, rows: (band, 0, 0, frame)),
+                pl.BlockSpec((1, stations, 2, 128), lambda band, rows: (band, 0, 0, 0)),
+                whole(first.shape),
+                whole(twiddle.shape),
+                whole(second.shape),
+            ],
+            out_specs=pl.BlockSpec((1, blocks, inner, 128), lambda band, rows: (band, 0, 0, 0)),
+            scratch_shapes=[
+                pltpu.VMEM((2, stations * STRIDE, 128), jnp.float32),
+                pltpu.VMEM((2 * RADIX_B * stations, 128), jnp.float32),
+            ],
+        ),
+        compiler_params=pltpu.CompilerParams(vmem_limit_bytes=48 * 2**20),
+        cost_estimate=pl.CostEstimate(
+            flops=4 * 10**9, bytes_accessed=10 * 2**20, transcendentals=0
+        ),
+    )(whole_rows, voltages, tail, filters, coarse, fine, first, twiddle, second)
+
+
+def exchange_kernel(sent_ref, got_ref, send_sem, recv_sem, own_sem):
+    times, groups = lax.axis_size("tm"), lax.axis_size("sta")
+    count = times * groups
+    at_time, at_group = lax.axis_index("tm"), lax.axis_index("sta")
+    me = at_time * groups + at_group
+    chunks = sent_ref.shape[0]
+    barrier = pltpu.get_barrier_semaphore()
+
+    def greet(step, carry):
+        other = lax.rem(me + step, count)
+        pl.semaphore_signal(
+            barrier, inc=1, device_id=(other // groups, lax.rem(other, groups)),
+            device_id_type=MESH,
+        )
+        return carry
+
+    lax.fori_loop(1, count, greet, 0)
+    pl.semaphore_wait(barrier, count - 1)
+    own = pltpu.make_async_copy(sent_ref.at[:, me], got_ref.at[:, me], own_sem)
+    own.start()
+    for chunk in range(chunks):
+
+        def send(step, carry, chunk=chunk):
+            other = lax.rem(me + step, count)
+            pltpu.make_async_remote_copy(
+                src_ref=sent_ref.at[chunk, other],
+                dst_ref=got_ref.at[chunk, me],
+                send_sem=send_sem.at[chunk],
+                recv_sem=recv_sem.at[chunk],
+                device_id=(other // groups, lax.rem(other, groups)),
+                device_id_type=MESH,
+            ).start()
+            return carry
+
+        lax.fori_loop(1, count, send, 0)
+    for chunk in range(chunks):
+        every = pltpu.make_async_remote_copy(
+            src_ref=sent_ref.at[chunk, pl.ds(0, count - 1)],
+            dst_ref=got_ref.at[chunk, pl.ds(0, count - 1)],
+            send_sem=send_sem.at[chunk],
+            recv_sem=recv_sem.at[chunk],
+            device_id=(at_time, at_group),
+            device_id_type=MESH,
+        )
+        every.wait_send()
+        every.wait_recv()
+    own.wait()
+
+
+def exchange(sent, collective):
+    return pl.pallas_call(
+        exchange_kernel,
+        out_shape=jax.ShapeDtypeStruct(sent.shape, sent.dtype),
+        in_specs=[pl.BlockSpec(memory_space=pl.ANY)],
+        out_specs=pl.BlockSpec(memory_space=pl.ANY),
+        scratch_shapes=[
+            pltpu.SemaphoreType.DMA((sent.shape[0],)),
+            pltpu.SemaphoreType.DMA((sent.shape[0],)),
+            pltpu.SemaphoreType.DMA,
+        ],
+        compiler_params=pltpu.CompilerParams(collective_id=collective, has_side_effects=True),
+        cost_estimate=pl.CostEstimate(
+            flops=0, bytes_accessed=300 * 2**20, transcendentals=0
+        ),
+    )(sent)
+
+
+def correlate_kernel(scale, *refs):
+    frame_refs, out_ref, turned = refs[:-2], refs[-2], refs[-1]
+    times, groups = frame_refs[0].shape[1], frame_refs[0].shape[2]
+    depth = 2 * times * len(frame_refs)
+    stations = groups * frame_refs[0].shape[5]
+    lane = lax.broadcasted_iota(jnp.int32, (128, 128), 1)
+    sign = jnp.where(lane < stations, 1.0, -1.0)
+    at = 0
+    for ref in frame_refs:
+        for time in range(times):
+            both = [
+                ref[0, time, group, 0, part] for part in range(2) for group in range(groups)
+            ]
+            tile = jnp.transpose(jnp.concatenate(both, axis=0).astype(jnp.float32))
+            turned[pl.ds(at, 128, stride=depth), :] = tile * sign
+            turned[pl.ds(depth // 2 + at, 128, stride=depth), :] = pltpu.roll(tile, stations, 1)
+            at += 1
+    many = 128 // depth
+
+    def step(group, carry):
+        rows = pl.ds(pl.multiple_of(group * 128, 128), 128)
+        block = turned[rows, :]
+        left = jnp.transpose(block)[:stations].astype(jnp.bfloat16)
+        narrow = block.astype(jnp.bfloat16)
+        columns = []
+        for one in range(many):
+            pieces = []
+            if one:
+                pieces.append(jnp.zeros((one * depth, 128), jnp.bfloat16))
+            pieces.append(narrow[one * depth : (one + 1) * depth])
+            if one < many - 1:
+                pieces.append(jnp.zeros(((many - 1 - one) * depth, 128), jnp.bfloat16))
+            columns.append(jnp.concatenate(pieces, axis=0))
+        result = jnp.dot(
+            left, jnp.concatenate(columns, axis=1), preferred_element_type=jnp.float32
+        )
+        for one in range(many):
+            out_ref[0, group * many + one] = result[:, one * 128 : (one + 1) * 128] * scale
+        return carry
+
+    lax.fori_loop(0, 128 // many, step, 0, unroll=4)
+
+
+def correlate_frames(frames, times, groups, stations):
+    bands, _, inner, _ = frames[0].shape
+    columns = inner // (2 * stations)
+    depth = 2 * times * len(frames)
+    shaped = [
+        frame.reshape(bands, times, groups, columns, 2, stations, 128) for frame in frames
+    ]
+    total = groups * stations
+    return pl.pallas_call(
+        functools.partial(correlate_kernel, 2.0 / depth),
+        out_shape=jax.ShapeDtypeStruct((bands, columns * 128, total, 2 * total), jnp.float32),
+        grid=(bands, columns),
+        in_specs=[
+            pl.BlockSpec(
+                (1, times, groups, 1, 2, stations, 128),
+                lambda band, column: (band, 0, 0, column, 0, 0, 0),
+            )
+            for _ in frames
+        ],
+        out_specs=pl.BlockSpec(
+            (1, 128, total, 2 * total), lambda band, column: (band, column, 0, 0)
+        ),
+        scratch_shapes=[pltpu.VMEM((128 * depth, 128), jnp.float32)],
+        compiler_params=pltpu.CompilerParams(vmem_limit_bytes=32 * 2**20),
+    )(*shaped)
+
+
+def flat_tables():
+    first, twiddle, second = dft_tables()
+    first = first.reshape(2 * RADIX_A, 2 * RADIX_A)
+    second = jnp.transpose(second, (1, 0, 2, 3)).reshape(2 * RADIX_B, 2 * RADIX_B)
+    return first, twiddle, second
+
+
+def local_narrow(voltages, sample_delay, frac_index, phase_index, fringe_rate):
+    stations, length = voltages.shape[2], voltages.shape[3]
+    times, groups = lax.axis_size("tm"), lax.axis_size("sta")
+    reach = REACH * 128
+    following = shifted(voltages[..., :reach], "tm", -1)
+    delay = sample_delay[:, 0]
+    filters = delay_filters(frac_index[:, 0], delay % 128)
+    coarse, fine = phasors(phase_index[:, :, 0], fringe_rate, length)
+    tables = flat_tables()
+    received = []
+    for frame in range(length // CHANNELS):
+        end = (frame + 1) * CHANNELS
+        tail = voltages[..., end : end + reach] if end + reach <= length else following
+        sent = station_spectra(
+            frame, voltages, tail, filters, coarse, fine, tables, delay // 128, times * groups
+        )
+        received.append(exchange(sent, frame))
+    return correlate_frames(received, times, groups, stations)
+
+
+def local(voltages, *others):
+    stations = voltages.shape[2] * lax.axis_size("sta")
+    block_width = CHANNELS // (lax.axis_size("tm") * lax.axis_size("sta"))
+    depth = 2 * lax.axis_size("tm") * (voltages.shape[3] // CHANNELS)
+    fits = voltages.shape[2] % 16 == 0 and block_width % 128 == 0 and depth <= 64
+    if fits and stations == 64:
+        return local_narrow(voltages, *others)
+    return local_wide(voltages, *others)
+
+
 def solution(mesh):
     return jax.shard_map(
         local,

time: 966 us -> 351 us (0.36); the launches traced: 949 us -> 350 us
  local copies, waits for them, and re-layouts: 486 us -> 8.6 us
  Pallas kernels: 0 us -> 320 us
  blocking collectives: 288 us -> 0 us
  matrix products: 81 us -> 0 us
  other arithmetic: 56.6 us -> 19.6 us
  waiting for transfers between devices: 34.7 us -> 0.01 us
    pallas_call x0 -> x5, Pallas kernels: none -> 320 us  [the longest x2 195 us: exchange(): pl.pallas_call(exchange_kernel, out_shape=jax.ShapeDtypeStruct(sent.shape...]
    all_to_all x2 -> x0, blocking collectives: 288 us -> none  [the longest x1 186 us: local(): lax.all_to_all(packed, 'tm', split_axis=3, concat_axis=2, tiled=True)]
    gather x192 -> x0, local copies, waits for them, and re-layouts: 235 us -> none
    dot_general x5 -> x0, matrix products: 81 us -> none  [the longest x1 43.3 us: correlate(): jnp.einsum('bifck,bjfck->bkij', spectra, partner, preferred_element_type=...]
    unnamed x20 -> x14, local copies, waits for them, and re-layouts: 84.5 us -> 4.42 us
    reshape x4 -> x0, local copies, waits for them, and re-layouts: 57.5 us -> none  [the longest x2 43.2 us: local(): received.reshape(band_count, station_count * groups, slices * frames, 2,...]
    another operation x5 -> x3, other arithmetic: 40.8 us -> 0.2 us  [the longest x1 0.12 us: phasors(): coarse = jnp.stack([jnp.cos(start_angle), jnp.sin(start_angle)], axis=2)]
    ppermute x1, waiting for transfers between devices: 34.7 us -> 0.01 us  [shifted(): lax.ppermute(value, axis, [(source, source + steps) for source in range(f...]
  transfers between devices with their start and end apart: 1 -> 1, of which waited for: 1 -> 0; matrix products, arithmetic and copies ran while one was open for 1% -> 6% of each run, Pallas kernels for 0% -> 36%
where the time goes in v1:
time: 351 us; the launch traced here: 350 us
  Pallas kernels  320 us (91%)
  other arithmetic  19.6 us (6%)
  local copies, waits for them, and re-layouts  8.6 us (2%)
    pallas_call x2, Pallas kernels, exchange(): pl.pallas_call(exchange_kernel, out_shape=jax.ShapeDtypeStruct(sent.shape...  195 us
    pallas_call x1, Pallas kernels, correlate_frames(): pl.pallas_call(functools.partial(correlate_kernel, 2.0 / depth), out_shap...  66.2 us
    pallas_call x2, Pallas kernels, station_spectra(): pl.pallas_call(station_kernel, out_shape=jax.ShapeDtypeStruct((bands, blo...  58.3 us
    convert_element_type x1, other arithmetic, delay_filters(): jnp.where(inside, jnp.sinc(centre) * window_taper, 0.0).astype(jnp.bfloat16)  15.1 us
  transfers between devices with their start and end apart: 1, of which 0 were waited for; matrix products, arithmetic and copies ran while one was open for 6% of the time, Pallas kernels for 36%

profile of v1, /device:TPU:11, one launch (start us, length us, event | category | flops | bytes accessed | tf_op | source)
XLA Modules:
  0.0 350.4 jit_solution(3717702285102804613)
XLA Ops:
  0.0 3.9 %fusion.46 = (bf16[2,4,16,8320]{3,2,1,0:T(8,128)(2,1)}, bf16[2,4,16,8320]{3,2,1,0:T(8,128)(2,1)S(1)}) fusion(bf16[2,4,16,32768]{3,2,1,0:T(8,128)(2,1)} %head_ref.3), kind=kLoop, calls=%fused_computation.85 | loop fusion | bytes 8519680 | tf_op jit(solution)/shard_map/slice | solution.py:460
  3.9 2.3 collective-permute-start
  6.2 0.3 fusion.41
  6.5 0.3 sine_multiply_fusion
  6.8 0.3 fusion.39
  7.1 0.0 copy-done.3
  7.2 0.1 copy.10
  7.3 0.1 copy.11
  7.5 0.0 copy-done.2
  7.5 1.1 fusion.43
  8.7 0.1 pad_maximum_fusion.2.fine_ref
  8.7 2.3 fusion.45
  11.0 0.1 pad_maximum_fusion.coarse_ref
  11.2 0.0 copy-done.4
  11.2 0.0 copy-done.5
  11.2 15.1 %select_convert_fusion.filter_ref = bf16[16,384,128]{2,1,0:T(8,128)(2,1)S(1)} fusion(f32[16]{0:T(128)S(1)} %multiply_bitcast_fusion, s32[16]{0:T(128)S(1)} %get-tuple-element.13, s32[384,128]{1,0:T(8,128)S(1)} %iota_subtract_fusion), kind=kLoop, calls=%fused_computation.29 | loop fusion | flops 36962304 | bytes 1769600 | tf_op jit(solution)/shard_map/convert_element_type | solution.py:188
  26.3 29.1 %shard_map.55.sent_ref = bf16[4,32,128,128]{3,2,1,0:T(8,128)(2,1)} custom-call(s32[16]{0:T(128)S(1)} %get-tuple-element.14.whole_rows, bf16[2,4,16,32768]{3,2,1,0:T(8,128)(2,1)} %head_ref.3, bf16[2,4,16,8320]{3,2,1,0:T(8,128)(2,1)S(1)} %get-tuple-element.6.tail_ref, bf16[16,384,128]{2,1,0:T(8,128)(2,1)S(1)} %select_convert_fusion.filter_ref, ...), custom_call_target="tpu_custom_call" | custom-call | flops 4000000000 | bytes 10485760 | tf_op jit(solution)/shard_map/pallas_call | solution.py:283
  55.4 98.1 %shard_map.56 = bf16[4,32,128,128]{3,2,1,0:T(8,128)(2,1)} custom-call(bf16[4,32,128,128]{3,2,1,0:T(8,128)(2,1)} %shard_map.55.sent_ref), custom_call_target="tpu_custom_call" | custom-call | bytes 314572800 | tf_op jit(solution)/shard_map/pallas_call | solution.py:362
  153.6 0.0 collective-permute-done.tail_ref
  153.6 29.2 %shard_map.57.sent_ref = bf16[4,32,128,128]{3,2,1,0:T(8,128)(2,1)} custom-call(s32[16]{0:T(128)S(1)} %get-tuple-element.14.whole_rows, bf16[2,4,16,32768]{3,2,1,0:T(8,128)(2,1)} %head_ref.3, bf16[2,4,16,8320]{3,2,1,0:T(8,128)(2,1)} %collective-permute-done.tail_ref, bf16[16,384,128]{2,1,0:T(8,128)(2,1)S(1)} %select_convert_fusion.filter_ref, ...), custom_call_target="tpu_custom_call" | custom-call | flops 4000000000 | bytes 10485760 | tf_op jit(solution)/shard_map/pallas_call | solution.py:283
  182.8 97.0 %shard_map.58 = bf16[4,32,128,128]{3,2,1,0:T(8,128)(2,1)} custom-call(bf16[4,32,128,128]{3,2,1,0:T(8,128)(2,1)} %shard_map.57.sent_ref), custom_call_target="tpu_custom_call" | custom-call | bytes 314572800 | tf_op jit(solution)/shard_map/pallas_call | solution.py:362
  279.8 2.2 copy-done
  282.0 2.2 copy-done.1
  284.2 66.2 %shard_map.59 = f32[4,512,64,128]{3,2,1,0:T(8,128)} custom-call(bf16[4,8,4,4,2,16,128]{6,5,4,3,2,1,0:T(8,128)(2,1)S(1)} %bitcast.37, bf16[4,8,4,4,2,16,128]{6,5,4,3,2,1,0:T(8,128)(2,1)S(1)} %bitcast.38), custom_call_target="tpu_custom_call" | custom-call | tf_op jit(solution)/shard_map/pallas_call | solution.py:430
  (19 shorter events, 0.2 us)
Async XLA Ops:
  0.0 7.2 %copy-start.3 = (s32[4,16,1]{1,2,0:T(1,128)S(1)}, s32[4,16,1]{1,2,0:T(1,128)}, u32[]{:S(2)}) copy-start(s32[4,16,1]{1,2,0:T(1,128)} %param.8) | copy-start | bytes 772
  0.0 7.5 %copy-start.2 = (f32[4,16]{1,0:T(4,128)S(1)}, f32[4,16]{1,0:T(4,128)}, u32[]{:S(2)}) copy-start(f32[4,16]{1,0:T(4,128)} %param.9) | copy-start | bytes 772
  3.9 7.3 %copy-start.4 = (s32[16,1]{0,1:T(1,128)S(1)}, s32[16,1]{0,1:T(1,128)}, u32[]{:S(2)}) copy-start(s32[16,1]{0,1:T(1,128)} %param.7) | copy-start | bytes 196
  3.9 7.3 %copy-start.5 = (s32[16,1]{0,1:T(1,128)S(1)}, s32[16,1]{0,1:T(1,128)}, u32[]{:S(2)}) copy-start(s32[16,1]{0,1:T(1,128)} %param.6) | copy-start | bytes 196
  3.9 149.7 %collective-permute-start = (bf16[2,4,16,8320]{3,2,1,0:T(8,128)(2,1)}, bf16[2,4,16,8320]{3,2,1,0:T(8,128)(2,1)}, u32[]{:S(2)}, u32[]{:S(2)}) collective-permute-start(bf16[2,4,16,8320]{3,2,1,0:T(8,128)(2,1)} %get-tuple-element.5), channel_id=1, source_target_pairs={{4,0},{8,4},{12,8},{16,12},{20,16},{24,20},{28,24},{5,1},{9,5},{13... | collective-permute-start | bytes 6389768 | tf_op jit(solution)/shard_map/ppermute | solution.py:24
  279.8 2.2 copy-start
  282.0 2.2 copy-start.1

commit v2 on v1

--- a/solution.py
+++ b/solution.py
@@ -173,19 +173,15 @@
 REACH = MAXD // 128 + 1
 STRIDE = ROWS + REACH + 7
 WINDOW = 384
+ABOVE = 128
+TALL = ABOVE + WINDOW
 MESH = pl.DeviceIdType.MESH
 
 
-def delay_filters(frac_index, remainder):
-    inputs_at = jnp.arange(WINDOW, dtype=jnp.int32)
-    outputs_at = jnp.arange(128, dtype=jnp.int32)
-    distance = inputs_at[None, :, None] - outputs_at[None, None, :] - remainder[:, None, None]
-    inside = (distance >= 0) & (distance < TAPS)
-    fraction = frac_index.astype(jnp.float32) / NFRAC
-    offset = distance.astype(jnp.float32)
-    centre = offset - (TAPS // 2 - 1) - fraction[:, None, None]
-    window_taper = 0.5 - 0.5 * jnp.cos(2.0 * jnp.pi * (offset + 0.5) / TAPS)
-    return jnp.where(inside, jnp.sinc(centre) * window_taper, 0.0).astype(jnp.bfloat16)
+def delay_filters(frac_index):
+    kernel = toeplitz_of(frac_index)[:, : 128 + TAPS].astype(jnp.float32)
+    kernel = jnp.pad(kernel, ((0, 0), (ABOVE, TALL - ABOVE - 128 - TAPS), (0, 0)))
+    return kernel.reshape(-1, 128)
 
 
 def phasors(phase_index, fringe_rate, length):
@@ -200,18 +196,13 @@
     return coarse, fine
 
 
-def station_kernel(
-    whole_rows, head_ref, tail_ref, filter_ref, coarse_ref, fine_ref, first_ref, twiddle_ref,
-    second_ref, out_ref, series, gathered
+def station_band(
+    shifts, read_head, read_tail, filter_ref, read_coarse, read_fine, first_ref, twiddle_ref,
+    second_ref, write, stations, blocks, series, gathered
 ):
-    stations = head_ref.shape[2]
-
     for part in range(2):
         for row in range(ROWS + REACH):
-            if row < ROWS:
-                tile = head_ref[part, 0, :, row * 128 : (row + 1) * 128]
-            else:
-                tile = tail_ref[part, 0, :, (row - ROWS) * 128 : (row - ROWS + 1) * 128]
+            tile = read_head(part, row) if row < ROWS else read_tail(part, row - ROWS)
             series[part, pl.ds(row, stations, stride=STRIDE), :] = tile.astype(jnp.float32)
         series[part, pl.ds(ROWS + REACH, stations, stride=STRIDE), :] = jnp.zeros(
             (stations, 128), jnp.float32
@@ -221,18 +212,20 @@
         return jnp.transpose(jnp.broadcast_to(row, (128, 128)))
 
     def one(station):
-        base = station * STRIDE + whole_rows[station]
+        base = station * STRIDE + shifts[0, station]
         parts = []
         for part in range(2):
             pieces = [
                 series[part, pl.ds(base + step, ROWS), :].astype(jnp.bfloat16) for step in range(3)
             ]
             parts.append(jnp.concatenate(pieces, axis=1))
+        taps = filter_ref[pl.ds(station * TALL + ABOVE - shifts[1, station], WINDOW), :]
         filtered = jnp.dot(
-            jnp.concatenate(parts, axis=0), filter_ref[station], preferred_element_type=jnp.float32
-        )
-        coarse = coarse_ref[0, station]
-        fine = fine_ref[0, station]
+            jnp.concatenate(parts, axis=0), taps.astype(jnp.bfloat16),
+            preferred_element_type=jnp.float32,
+        )
+        coarse = read_coarse(station)
+        fine = read_fine(station)
         cos_a, sin_a = across(coarse[0:1]), across(coarse[1:2])
         cos_b, sin_b = fine[0:1], fine[1:2]
         cosine = cos_a * cos_b - sin_a * sin_b
@@ -265,17 +258,47 @@
         return carry
 
     lax.fori_loop(0, stations // 2, pair, 0)
-    blocks, inner = out_ref.shape[1], out_ref.shape[2]
+    inner = 2 * RADIX_B // blocks * stations
 
     def pack(block, carry):
         rows = pl.ds(pl.multiple_of(block * inner, inner), inner)
-        out_ref[0, block] = gathered[rows, :].astype(jnp.bfloat16)
+        write(block, gathered[rows, :].astype(jnp.bfloat16))
         return carry
 
     lax.fori_loop(0, blocks, pack, 0)
 
 
-def station_spectra(frame, voltages, tail, filters, coarse, fine, tables, whole_rows, blocks):
+def columns_of(row):
+    return slice(row * 128, (row + 1) * 128)
+
+
+def station_kernel(
+    shifts, head_ref, tail_ref, filter_ref, coarse_ref, fine_ref, first_ref, twiddle_ref,
+    second_ref, out_ref, series, gathered
+):
+    def write(block, value):
+        out_ref[0, block] = value
+
+    station_band(
+        shifts,
+        lambda part, row: head_ref[part, 0, :, columns_of(row)],
+        lambda part, row: tail_ref[part, 0, :, columns_of(row)],
+        filter_ref,
+        lambda station: coarse_ref[0, station],
+        lambda station: fine_ref[0, station],
+        first_ref, twiddle_ref, second_ref, write,
+        head_ref.shape[2], out_ref.shape[1], series, gathered,
+    )
+
+
+def station_scratch(stations):
+    return [
+        pltpu.VMEM((2, stations * STRIDE, 128), jnp.float32),
+        pltpu.VMEM((2 * RADIX_B * stations, 128), jnp.float32),
+    ]
+
+
+def station_spectra(voltages, shifts, tail, filters, coarse, fine, tables, blocks):
     _, bands, stations, _ = voltages.shape
     first, twiddle, second = tables
     inner = 2 * RADIX_B // blocks * stations
@@ -287,34 +310,36 @@
             num_scalar_prefetch=1,
             grid=(bands,),
             in_specs=[
-                pl.BlockSpec((2, 1, stations, CHANNELS), lambda band, rows: (0, band, 0, frame)),
+                pl.BlockSpec((2, 1, stations, CHANNELS), lambda band, rows: (0, band, 0, 0)),
                 pl.BlockSpec((2, 1, stations, REACH * 128), lambda band, rows: (0, band, 0, 0)),
                 whole(filters.shape),
-                pl.BlockSpec((1, stations, 2, 128), lambda band, rows: (band, 0, 0, frame)),
+                pl.BlockSpec((1, stations, 2, 128), lambda band, rows: (band, 0, 0, 0)),
                 pl.BlockSpec((1, stations, 2, 128), lambda band, rows: (band, 0, 0, 0)),
                 whole(first.shape),
                 whole(twiddle.shape),
                 whole(second.shape),
             ],
             out_specs=pl.BlockSpec((1, blocks, inner, 128), lambda band, rows: (band, 0, 0, 0)),
-            scratch_shapes=[
-                pltpu.VMEM((2, stations * STRIDE, 128), jnp.float32),
-                pltpu.VMEM((2 * RADIX_B * stations, 128), jnp.float32),
-            ],
+            scratch_shapes=station_scratch(stations),
         ),
         compiler_params=pltpu.CompilerParams(vmem_limit_bytes=48 * 2**20),
         cost_estimate=pl.CostEstimate(
             flops=4 * 10**9, bytes_accessed=10 * 2**20, transcendentals=0
         ),
-    )(whole_rows, voltages, tail, filters, coarse, fine, first, twiddle, second)
-
-
-def exchange_kernel(sent_ref, got_ref, send_sem, recv_sem, own_sem):
+    )(shifts, voltages, tail, filters, coarse, fine, first, twiddle, second)
+
+
+def stream_kernel(
+    shifts, voltages_ref, tail_ref, sent_ref, filter_ref, coarse_ref, fine_ref, first_ref,
+    twiddle_ref, second_ref, got_ref, last_ref, heads, tails, ready, series, gathered,
+    send_sem, recv_sem, own_sem, load_sem
+):
     times, groups = lax.axis_size("tm"), lax.axis_size("sta")
     count = times * groups
     at_time, at_group = lax.axis_index("tm"), lax.axis_index("sta")
     me = at_time * groups + at_group
-    chunks = sent_ref.shape[0]
+    bands = sent_ref.shape[0]
+    stations = heads.shape[2]
     barrier = pltpu.get_barrier_semaphore()
 
     def greet(step, carry):
@@ -325,29 +350,68 @@
         )
         return carry
 
+    load_head = pltpu.make_async_copy(
+        voltages_ref.at[:, :, :, pl.ds(CHANNELS, CHANNELS)], heads, load_sem.at[0]
+    )
+    load_tail = pltpu.make_async_copy(tail_ref, tails, load_sem.at[1])
+    load_head.start()
+    load_tail.start()
     lax.fori_loop(1, count, greet, 0)
     pl.semaphore_wait(barrier, count - 1)
-    own = pltpu.make_async_copy(sent_ref.at[:, me], got_ref.at[:, me], own_sem)
+
+    def copy_to(other, source, target, chunk):
+        return pltpu.make_async_remote_copy(
+            src_ref=source,
+            dst_ref=target,
+            send_sem=send_sem.at[chunk],
+            recv_sem=recv_sem.at[chunk],
+            device_id=(other // groups, lax.rem(other, groups)),
+            device_id_type=MESH,
+        )
+
+    def send_all(source, target, band, chunk):
+        def send(step, carry):
+            other = lax.rem(me + step, count)
+            copy_to(other, source.at[band, other], target.at[band, me], chunk).start()
+            return carry
+
+        lax.fori_loop(1, count, send, 0)
+
+    def first_frame(band, carry):
+        send_all(sent_ref, got_ref, band, band)
+        return carry
+
+    lax.fori_loop(0, bands, first_frame, 0)
+    own = pltpu.make_async_copy(sent_ref.at[:, me], got_ref.at[:, me], own_sem.at[0])
     own.start()
-    for chunk in range(chunks):
-
-        def send(step, carry, chunk=chunk):
-            other = lax.rem(me + step, count)
-            pltpu.make_async_remote_copy(
-                src_ref=sent_ref.at[chunk, other],
-                dst_ref=got_ref.at[chunk, me],
-                send_sem=send_sem.at[chunk],
-                recv_sem=recv_sem.at[chunk],
-                device_id=(other // groups, lax.rem(other, groups)),
-                device_id_type=MESH,
-            ).start()
-            return carry
-
-        lax.fori_loop(1, count, send, 0)
-    for chunk in range(chunks):
+    load_head.wait()
+    load_tail.wait()
+
+    def second_frame(band, carry):
+        def write(block, value):
+            ready[band, block] = value
+
+        station_band(
+            shifts,
+            lambda part, row: heads[part, band, :, columns_of(row)],
+            lambda part, row: tails[part, band, :, columns_of(row)],
+            filter_ref,
+            lambda station: coarse_ref[band, station],
+            lambda station: fine_ref[band, station],
+            first_ref, twiddle_ref, second_ref, write,
+            stations, count, series, gathered,
+        )
+        send_all(ready, last_ref, band, bands + band)
+        return carry
+
+    lax.fori_loop(0, bands, second_frame, 0)
+    own_last = pltpu.make_async_copy(ready.at[:, me], last_ref.at[:, me], own_sem.at[1])
+    own_last.start()
+    for chunk in range(2 * bands):
+        source, target = (sent_ref, got_ref) if chunk < bands else (ready, last_ref)
         every = pltpu.make_async_remote_copy(
-            src_ref=sent_ref.at[chunk, pl.ds(0, count - 1)],
-            dst_ref=got_ref.at[chunk, pl.ds(0, count - 1)],
+            src_ref=source.at[chunk % bands, pl.ds(0, count - 1)],
+            dst_ref=target.at[chunk % bands, pl.ds(0, count - 1)],
             send_sem=send_sem.at[chunk],
             recv_sem=recv_sem.at[chunk],
             device_id=(at_time, at_group),
@@ -356,67 +420,82 @@
         every.wait_send()
         every.wait_recv()
     own.wait()
-
-
-def exchange(sent, collective):
+    own_last.wait()
+
+
+def stream(shifts, voltages, tail, sent, filters, coarse, fine, tables):
+    _, bands, stations, _ = voltages.shape
+    inside = pl.BlockSpec(memory_space=pltpu.VMEM)
+    outside = pl.BlockSpec(memory_space=pl.ANY)
+    shape = jax.ShapeDtypeStruct(sent.shape, sent.dtype)
     return pl.pallas_call(
-        exchange_kernel,
-        out_shape=jax.ShapeDtypeStruct(sent.shape, sent.dtype),
-        in_specs=[pl.BlockSpec(memory_space=pl.ANY)],
-        out_specs=pl.BlockSpec(memory_space=pl.ANY),
+        stream_kernel,
+        out_shape=(shape, shape),
+        in_specs=[pl.BlockSpec(memory_space=pltpu.SMEM)] + [outside] * 3 + [inside] * 6,
+        out_specs=(outside, outside),
         scratch_shapes=[
-            pltpu.SemaphoreType.DMA((sent.shape[0],)),
-            pltpu.SemaphoreType.DMA((sent.shape[0],)),
-            pltpu.SemaphoreType.DMA,
+            pltpu.VMEM((2, bands, stations, CHANNELS), voltages.dtype),
+            pltpu.VMEM(tail.shape, tail.dtype),
+            pltpu.VMEM(sent.shape, sent.dtype),
+        ]
+        + station_scratch(stations)
+        + [
+            pltpu.SemaphoreType.DMA((2 * bands,)),
+            pltpu.SemaphoreType.DMA((2 * bands,)),
+            pltpu.SemaphoreType.DMA((2,)),
+            pltpu.SemaphoreType.DMA((2,)),
         ],
-        compiler_params=pltpu.CompilerParams(collective_id=collective, has_side_effects=True),
+        compiler_params=pltpu.CompilerParams(
+            collective_id=0, has_side_effects=True, vmem_limit_bytes=48 * 2**20
+        ),
         cost_estimate=pl.CostEstimate(
-            flops=0, bytes_accessed=300 * 2**20, transcendentals=0
-        ),
-    )(sent)
+            flops=4 * 10**9, bytes_accessed=600 * 2**20, transcendentals=0
+        ),
+    )(shifts, voltages, tail, sent, filters, coarse, fine, *tables)
 
 
 def correlate_kernel(scale, *refs):
     frame_refs, out_ref, turned = refs[:-2], refs[-2], refs[-1]
     times, groups = frame_refs[0].shape[1], frame_refs[0].shape[2]
-    depth = 2 * times * len(frame_refs)
+    frames = times * len(frame_refs)
     stations = groups * frame_refs[0].shape[5]
-    lane = lax.broadcasted_iota(jnp.int32, (128, 128), 1)
-    sign = jnp.where(lane < stations, 1.0, -1.0)
+    stride = frames + 8
     at = 0
     for ref in frame_refs:
         for time in range(times):
             both = [
                 ref[0, time, group, 0, part] for part in range(2) for group in range(groups)
             ]
-            tile = jnp.transpose(jnp.concatenate(both, axis=0).astype(jnp.float32))
-            turned[pl.ds(at, 128, stride=depth), :] = tile * sign
-            turned[pl.ds(depth // 2 + at, 128, stride=depth), :] = pltpu.roll(tile, stations, 1)
+            turned[pl.ds(at, 128, stride=stride), :] = jnp.transpose(
+                jnp.concatenate(both, axis=0).astype(jnp.float32)
+            )
             at += 1
-    many = 128 // depth
+    many = 128 // frames
+    lane = lax.broadcasted_iota(jnp.int32, (128, 128), 1)
+    sign = jnp.where(lane < stations, 1.0, -1.0).astype(jnp.bfloat16)
+    owner = lax.broadcasted_iota(jnp.int32, (stations, 256), 1) % 128 // frames
 
     def step(group, carry):
-        rows = pl.ds(pl.multiple_of(group * 128, 128), 128)
-        block = turned[rows, :]
-        left = jnp.transpose(block)[:stations].astype(jnp.bfloat16)
-        narrow = block.astype(jnp.bfloat16)
-        columns = []
+        block = jnp.concatenate(
+            [
+                turned[pl.ds(pl.multiple_of((group * many + one) * stride, 8), frames), :]
+                for one in range(many)
+            ],
+            axis=0,
+        ).astype(jnp.bfloat16)
+        flipped = jnp.transpose(block)
+        left = jnp.concatenate([flipped[:stations], flipped[stations:]], axis=1)
+        swapped = jnp.concatenate([block[:, stations:], block[:, :stations]], axis=1)
+        right = jnp.concatenate([block * sign, swapped], axis=0)
+        spread = jnp.concatenate(
+            [jnp.where(owner == one, left, jnp.zeros_like(left)) for one in range(many)], axis=0
+        )
+        result = jnp.dot(spread, right, preferred_element_type=jnp.float32)
         for one in range(many):
-            pieces = []
-            if one:
-                pieces.append(jnp.zeros((one * depth, 128), jnp.bfloat16))
-            pieces.append(narrow[one * depth : (one + 1) * depth])
-            if one < many - 1:
-                pieces.append(jnp.zeros(((many - 1 - one) * depth, 128), jnp.bfloat16))
-            columns.append(jnp.concatenate(pieces, axis=0))
-        result = jnp.dot(
-            left, jnp.concatenate(columns, axis=1), preferred_element_type=jnp.float32
-        )
-        for one in range(many):
-            out_ref[0, group * many + one] = result[:, one * 128 : (one + 1) * 128] * scale
+            out_ref[0, group * many + one] = result[one * stations : (one + 1) * stations] * scale
         return carry
 
-    lax.fori_loop(0, 128 // many, step, 0, unroll=4)
+    lax.fori_loop(0, 128 // many, step, 0, unroll=True)
 
 
 def correlate_frames(frames, times, groups, stations):
@@ -441,7 +520,7 @@
         out_specs=pl.BlockSpec(
             (1, 128, total, 2 * total), lambda band, column: (band, column, 0, 0)
         ),
-        scratch_shapes=[pltpu.VMEM((128 * depth, 128), jnp.float32)],
+        scratch_shapes=[pltpu.VMEM((128 * (depth // 2 + 8), 128), jnp.float32)],
         compiler_params=pltpu.CompilerParams(vmem_limit_bytes=32 * 2**20),
     )(*shaped)
 
@@ -454,31 +533,30 @@
 
 
 def local_narrow(voltages, sample_delay, frac_index, phase_index, fringe_rate):
-    stations, length = voltages.shape[2], voltages.shape[3]
+    length = voltages.shape[3]
     times, groups = lax.axis_size("tm"), lax.axis_size("sta")
     reach = REACH * 128
     following = shifted(voltages[..., :reach], "tm", -1)
     delay = sample_delay[:, 0]
-    filters = delay_filters(frac_index[:, 0], delay % 128)
+    shifts = jnp.stack([delay // 128, delay % 128])
+    filters = delay_filters(frac_index[:, 0])
     coarse, fine = phasors(phase_index[:, :, 0], fringe_rate, length)
     tables = flat_tables()
-    received = []
-    for frame in range(length // CHANNELS):
-        end = (frame + 1) * CHANNELS
-        tail = voltages[..., end : end + reach] if end + reach <= length else following
-        sent = station_spectra(
-            frame, voltages, tail, filters, coarse, fine, tables, delay // 128, times * groups
-        )
-        received.append(exchange(sent, frame))
-    return correlate_frames(received, times, groups, stations)
+    middle = voltages[..., CHANNELS : CHANNELS + reach]
+    early, late = coarse[..., :ROWS], coarse[..., ROWS:]
+    sent = station_spectra(
+        voltages, shifts, middle, filters, early, fine, tables, times * groups
+    )
+    received = stream(shifts, voltages, following, sent, filters, late, fine, tables)
+    return correlate_frames(received, times, groups, voltages.shape[2])
 
 
 def local(voltages, *others):
     stations = voltages.shape[2] * lax.axis_size("sta")
     block_width = CHANNELS // (lax.axis_size("tm") * lax.axis_size("sta"))
     depth = 2 * lax.axis_size("tm") * (voltages.shape[3] // CHANNELS)
-    fits = voltages.shape[2] % 16 == 0 and block_width % 128 == 0 and depth <= 64
-    if fits and stations == 64:
+    fits = voltages.shape[2] % 16 == 0 and block_width % 128 == 0 and depth == 32
+    if fits and stations == 64 and voltages.shape[3] == 2 * CHANNELS:
         return local_narrow(voltages, *others)
     return local_wide(voltages, *others)
 

time: 351 us -> 278 us (0.79)
  Pallas kernels: 320 us -> 252 us
  other arithmetic: 19.6 us -> 10.5 us
  waiting for transfers between devices: 0.01 us -> 5.72 us
    pallas_call x1, Pallas kernels: 66.2 us -> 30.2 us  [correlate_frames(): pl.pallas_call(functools.partial(correlate_kernel, 2.0 / depth), out_shap...]
    pallas_call x2 -> x1, Pallas kernels: 58.3 us -> 30.7 us  [station_spectra(): pl.pallas_call(station_kernel, out_shape=jax.ShapeDtypeStruct((bands, blo...]
    convert_element_type x1, other arithmetic: 15.1 us -> 0.46 us  [toeplitz_of(): return jnp.where(inside[None, :, :], values, 0.0).astype(jnp.bfloat16)]
    ppermute x1, waiting for transfers between devices: 0.01 us -> 5.72 us  [shifted(): lax.ppermute(value, axis, [(source, source + steps) for source in range(f...]
    pallas_call x2 -> x1, Pallas kernels: 195 us -> 191 us  [stream(): pl.pallas_call(stream_kernel, out_shape=(shape, shape), in_specs=[pl.Bloc...]
  transfers between devices with their start and end apart: 1 -> 1, of which waited for: 0 -> 1; matrix products, arithmetic and copies ran while one was open for 6% -> 4% of each run, Pallas kernels for 36% -> 11%
where the time goes in v2:
time: 278 us
  Pallas kernels  252 us (91%)
  other arithmetic  10.5 us (4%)
  local copies, waits for them, and re-layouts  7.61 us (3%)
  waiting for transfers between devices  5.72 us (2%)
    pallas_call x1, Pallas kernels, stream(): pl.pallas_call(stream_kernel, out_shape=(shape, shape), in_specs=[pl.Bloc...  191 us
    pallas_call x1, Pallas kernels, station_spectra(): pl.pallas_call(station_kernel, out_shape=jax.ShapeDtypeStruct((bands, blo...  30.7 us
    pallas_call x1, Pallas kernels, correlate_frames(): pl.pallas_call(functools.partial(correlate_kernel, 2.0 / depth), out_shap...  30.2 us
    ppermute x1, waiting for transfers between devices, shifted(): lax.ppermute(value, axis, [(source, source + steps) for source in range(f...  5.72 us
  transfers between devices with their start and end apart: 1, of which 1 were waited for; matrix products, arithmetic and copies ran while one was open for 4% of the time, Pallas kernels for 11%

profile of v2, /device:TPU:11, one launch (start us, length us, event | category | flops | bytes accessed | tf_op | source)
XLA Modules:
  0.0 277.8 jit_solution(5721357623668394786)
XLA Ops:
  0.0 2.5 fusion.36
  2.5 2.2 collective-permute-start
  4.7 0.3 fusion.31
  5.0 0.3 sine_multiply_fusion
  5.4 0.5 multiply_subtract_fusion
  5.9 0.3 fusion.29
  6.2 0.5 fusion.2
  6.7 0.0 copy-start.3
  6.7 0.0 copy-start.2
  6.7 2.1 fusion.7
  8.9 0.1 copy.10
  9.0 0.1 copy.11
  9.3 1.1 fusion.33
  10.4 2.3 fusion.34
  12.7 0.5 fusion.12
  13.2 0.4 pad.5
  13.5 0.2 pad_maximum_fusion.1
  13.7 2.4 bitcast_convert_fusion.filter_ref
  16.1 30.7 %shard_map.55.sent_ref = bf16[4,32,128,128]{3,2,1,0:T(8,128)(2,1)} custom-call(s32[2,16]{1,0:T(2,128)S(1)} %pad_add_fusion.shifts, bf16[2,4,16,32768]{3,2,1,0:T(8,128)(2,1)} %voltages_ref.1, bf16[2,4,16,8320]{3,2,1,0:T(8,128)(2,1)S(1)} %get-tuple-element.9.tail_ref, f32[8192,128]{1,0:T(8,128)} %bitcast_convert_fusion.filter_ref, ...), custom_call_target="tpu_custom_call" | custom-call | flops 4000000000 | bytes 10485760 | tf_op jit(solution)/shard_map/pallas_call | solution.py:306
  46.8 5.7 %collective-permute-done.tail_ref = bf16[2,4,16,8320]{3,2,1,0:T(8,128)(2,1)S(1)} collective-permute-done((bf16[2,4,16,8320]{3,2,1,0:T(8,128)(2,1)S(1)}, bf16[2,4,16,8320]{3,2,1,0:T(8,128)(2,1)S(1)}, u32[]{:S(2)}, u32[]{:S(2)}) %collective-permute-start) | collective-permute-done | bytes 2129952 | tf_op jit(solution)/shard_map/ppermute | solution.py:24
  52.5 190.8 %shard_map.56 = (bf16[4,32,128,128]{3,2,1,0:T(8,128)(2,1)}, bf16[4,32,128,128]{3,2,1,0:T(8,128)(2,1)}) custom-call(s32[2,16]{1,0:T(2,128)S(1)} %pad_add_fusion.shifts, bf16[2,4,16,32768]{3,2,1,0:T(8,128)(2,1)} %voltages_ref.1, bf16[2,4,16,8320]{3,2,1,0:T(8,128)(2,1)S(1)} %collective-permute-done.tail_ref, bf16[4,32,128,128]{3,2,1,0:T(8,128)(2,1)} %shard_map.55.sent_ref, ...), custom_call_target="tpu_custom_call" | custom-call | flops 4000000000 | bytes 629145600 | tf_op jit(solution)/shard_map/pallas_call | solution.py:431
  243.3 2.2 copy-done
  245.5 2.2 copy-done.1
  247.7 30.2 %shard_map.57 = f32[4,512,64,128]{3,2,1,0:T(8,128)} custom-call(bf16[4,8,4,4,2,16,128]{6,5,4,3,2,1,0:T(8,128)(2,1)S(1)} %bitcast.40, bf16[4,8,4,4,2,16,128]{6,5,4,3,2,1,0:T(8,128)(2,1)S(1)} %bitcast.41), custom_call_target="tpu_custom_call" | custom-call | tf_op jit(solution)/shard_map/pallas_call | solution.py:509
  (25 shorter events, 0.2 us)
Async XLA Ops:
  0.0 6.2 %copy-start.4 = (s32[16,1]{0,1:T(1,128)S(1)}, s32[16,1]{0,1:T(1,128)}, u32[]{:S(2)}) copy-start(s32[16,1]{0,1:T(1,128)} %param.7) | copy-start | bytes 196
  2.5 50.0 %collective-permute-start = (bf16[2,4,16,8320]{3,2,1,0:T(8,128)(2,1)S(1)}, bf16[2,4,16,8320]{3,2,1,0:T(8,128)(2,1)S(1)}, u32[]{:S(2)}, u32[]{:S(2)}) collective-permute-start(bf16[2,4,16,8320]{3,2,1,0:T(8,128)(2,1)S(1)} %get-tuple-element.10), channel_id=1, source_target_pairs={{4,0},{8,4},{12,8},{16,12},{20,16},{24,20},{28,24},{5,1},{9,5},{13... | collective-permute-start | bytes 6389768 | tf_op jit(solution)/shard_map/ppermute | solution.py:24
  6.7 2.1 copy-start.5
  6.7 2.2 copy-start.3
  6.7 2.6 copy-start.2
  243.3 2.2 copy-start
  245.5 2.2 copy-start.1

commit v3 on v2

--- a/solution.py
+++ b/solution.py
@@ -521,7 +521,7 @@
             (1, 128, total, 2 * total), lambda band, column: (band, column, 0, 0)
         ),
         scratch_shapes=[pltpu.VMEM((128 * (depth // 2 + 8), 128), jnp.float32)],
-        compiler_params=pltpu.CompilerParams(vmem_limit_bytes=32 * 2**20),
+        compiler_params=pltpu.CompilerParams(vmem_limit_bytes=58 * 2**20),
     )(*shaped)
 
 

time: 278 us -> 274 us (0.986)
  local copies, waits for them, and re-layouts: 7.61 us -> 3.24 us
    unnamed x14 -> x10, local copies, waits for them, and re-layouts: 4.43 us -> 0.06 us
where the time goes in v3:
time: 274 us
  Pallas kernels  252 us (92%)
  other arithmetic  10.5 us (4%)
  waiting for transfers between devices  5.58 us (2%)
  local copies, waits for them, and re-layouts  3.24 us (1%)
    pallas_call x1, Pallas kernels, stream(): pl.pallas_call(stream_kernel, out_shape=(shape, shape), in_specs=[pl.Bloc...  191 us
    pallas_call x1, Pallas kernels, correlate_frames(): pl.pallas_call(functools.partial(correlate_kernel, 2.0 / depth), out_shap...  30.9 us
    pallas_call x1, Pallas kernels, station_spectra(): pl.pallas_call(station_kernel, out_shape=jax.ShapeDtypeStruct((bands, blo...  30.8 us
    ppermute x1, waiting for transfers between devices, shifted(): lax.ppermute(value, axis, [(source, source + steps) for source in range(f...  5.58 us
  transfers between devices with their start and end apart: 1, of which 1 were waited for; matrix products, arithmetic and copies ran while one was open for 4% of the time, Pallas kernels for 11%

profile of v3, /device:TPU:11, one launch (start us, length us, event | category | flops | bytes accessed | tf_op | source)
XLA Modules:
  0.0 274.2 jit_solution(13737774245096021756)
XLA Ops:
  0.0 2.5 fusion.36
  2.5 2.2 collective-permute-start
  4.7 0.3 fusion.31
  5.0 0.3 sine_multiply_fusion
  5.4 0.5 multiply_subtract_fusion
  5.9 0.3 fusion.29
  6.2 0.0 copy-done.2
  6.2 0.5 fusion.2
  6.7 0.0 copy-start.3
  6.7 0.0 copy-start.1
  6.7 0.0 copy-start
  6.7 2.1 fusion.7
  8.9 0.1 copy.10
  9.0 0.1 copy.11
  9.3 1.1 fusion.33
  10.4 2.3 fusion.34
  12.7 0.5 fusion.12
  13.2 0.4 pad.5
  13.5 0.2 pad_maximum_fusion.1
  13.7 2.4 bitcast_convert_fusion.filter_ref
  16.1 30.8 %shard_map.55.sent_ref = bf16[4,32,128,128]{3,2,1,0:T(8,128)(2,1)} custom-call(s32[2,16]{1,0:T(2,128)S(1)} %pad_add_fusion.shifts, bf16[2,4,16,32768]{3,2,1,0:T(8,128)(2,1)} %voltages_ref.1, bf16[2,4,16,8320]{3,2,1,0:T(8,128)(2,1)S(1)} %get-tuple-element.9.tail_ref, f32[8192,128]{1,0:T(8,128)} %bitcast_convert_fusion.filter_ref, ...), custom_call_target="tpu_custom_call" | custom-call | flops 4000000000 | bytes 10485760 | tf_op jit(solution)/shard_map/pallas_call | solution.py:306
  47.0 5.6 %collective-permute-done.tail_ref = bf16[2,4,16,8320]{3,2,1,0:T(8,128)(2,1)S(1)} collective-permute-done((bf16[2,4,16,8320]{3,2,1,0:T(8,128)(2,1)S(1)}, bf16[2,4,16,8320]{3,2,1,0:T(8,128)(2,1)S(1)}, u32[]{:S(2)}, u32[]{:S(2)}) %collective-permute-start) | collective-permute-done | bytes 2129952 | tf_op jit(solution)/shard_map/ppermute | solution.py:24
  52.5 190.8 %shard_map.56 = (bf16[4,32,128,128]{3,2,1,0:T(8,128)(2,1)}, bf16[4,32,128,128]{3,2,1,0:T(8,128)(2,1)}) custom-call(s32[2,16]{1,0:T(2,128)S(1)} %pad_add_fusion.shifts, bf16[2,4,16,32768]{3,2,1,0:T(8,128)(2,1)} %voltages_ref.1, bf16[2,4,16,8320]{3,2,1,0:T(8,128)(2,1)S(1)} %collective-permute-done.tail_ref, bf16[4,32,128,128]{3,2,1,0:T(8,128)(2,1)} %shard_map.55.sent_ref, ...), custom_call_target="tpu_custom_call" | custom-call | flops 4000000000 | bytes 629145600 | tf_op jit(solution)/shard_map/pallas_call | solution.py:431
  243.3 30.9 %shard_map.57 = f32[4,512,64,128]{3,2,1,0:T(8,128)} custom-call(bf16[4,8,4,4,2,16,128]{6,5,4,3,2,1,0:T(8,128)(2,1)} %bitcast.44, bf16[4,8,4,4,2,16,128]{6,5,4,3,2,1,0:T(8,128)(2,1)} %bitcast.45), custom_call_target="tpu_custom_call" | custom-call | tf_op jit(solution)/shard_map/pallas_call | solution.py:509
  (21 shorter events, 0.2 us)
Async XLA Ops:
  0.0 6.2 %copy-start.2 = (s32[16,1]{0,1:T(1,128)S(1)}, s32[16,1]{0,1:T(1,128)}, u32[]{:S(2)}) copy-start(s32[16,1]{0,1:T(1,128)} %param.7) | copy-start | bytes 196
  2.5 50.0 %collective-permute-start = (bf16[2,4,16,8320]{3,2,1,0:T(8,128)(2,1)S(1)}, bf16[2,4,16,8320]{3,2,1,0:T(8,128)(2,1)S(1)}, u32[]{:S(2)}, u32[]{:S(2)}) collective-permute-start(bf16[2,4,16,8320]{3,2,1,0:T(8,128)(2,1)S(1)} %get-tuple-element.10), channel_id=1, source_target_pairs={{4,0},{8,4},{12,8},{16,12},{20,16},{24,20},{28,24},{5,1},{9,5},{13... | collective-permute-start | bytes 6389768 | tf_op jit(solution)/shard_map/ppermute | solution.py:24
  6.7 2.1 copy-start.3
  6.7 2.2 copy-start.1
  6.7 2.6 copy-start
